TPU v7x, 32 devices: a whole 2x2x4 slice. The times are simulated.
32 devices in a mesh: prow: 4 (over x, core), pcol: 8 (over z, y).
Axes of the slice: x: 2, y: 2, z: 4, core: 2. Of those that a mesh axis runs over, the one named last changes fastest.
Arguments:
- blocks: bfloat16 [20480, 128, 128], P(('prow', 'pcol')), may hold values from -0.078125 to 0.078125
- row_index: int32 [20480], P(('prow', 'pcol')), may hold values from 0 to 511, as said below
- col_index: int32 [20480], P(('prow', 'pcol')), may hold values from 0 to 511, as said below
- send_tiles: int32 [512], P(('prow', 'pcol')), may hold values from 0 to 511, as said below
- lighting: bfloat16 [65536, 384], P(('prow', 'pcol')), may hold values from -6 to 6
- albedo: float32 [3, 65536], P(None, ('pcol', 'prow')), may hold values from 0.2 to 0.95
- emission: bfloat16 [65536, 384], P(('pcol', 'prow')), may hold values from -4 to 4
Outputs:
- radiance: bfloat16 [65536, 384], P(('pcol', 'prow'))
Inputs may be any that keep to these rules, and one draw needn't show every extreme that they name: `send_tiles`: group g (the blocks of device g) lists 16 distinct tiles in increasing order: exactly 4 from each of the 4 ranges of 16 block rows starting at c * 64 + r * 16, r = 0 .. 3, where c = g % 8. `row_index`: each block's row is one of its group's listed tiles, each listed tile has at least one block, and a group's blocks are ordered by row; counts per tile are uneven. `col_index`: the blocks of group g have columns in (g // 8) * 128 to (g // 8 + 1) * 128 - 1; a pair of row and column may repeat, and then the blocks add.
All inputs are finite; a program needn't handle non-finite values.
Results may differ from a plain program's by a relative error of at most 0.008.
Values may be sent and summed in bfloat16 or wider, within the bound.
A program may use at most 192 MiB of HBM per device.

v0:
```python
import math

import jax
import jax.numpy as jnp
from jax import lax
from jax.sharding import PartitionSpec as P


def per_device(blocks, row_index, col_index, send_tiles, lighting, albedo, emission):
    tile_size = blocks.shape[1]
    col_width = lighting.shape[1]
    block_count = blocks.shape[0]
    list_count = send_tiles.shape[0]
    prow_count = lax.axis_size("prow")
    own_count = emission.shape[0] // tile_size
    strip_rows = own_count * prow_count
    prow_here = lax.axis_index("prow")
    pcol_here = lax.axis_index("pcol")
    slab = lax.all_gather(lighting, "pcol", axis=0, tiled=True)
    slab_count = slab.shape[0] // tile_size
    slab_flat = slab.reshape(slab_count, tile_size * col_width)
    local_cols = col_index - prow_here * slab_count
    slots = jnp.sum((send_tiles[None, :] < row_index[:, None]).astype(jnp.int32), axis=1)
    group_size = math.gcd(block_count, 64)
    group_total = block_count // group_size
    list_iota = jnp.arange(list_count, dtype=jnp.int32)

    def one_group(running, items):
        block_set, col_set, slot_set = items
        picked = jnp.take(slab_flat, col_set, axis=0).reshape(group_size, tile_size, col_width)
        product = jnp.einsum("gpq,gqk->gpk", block_set, picked, preferred_element_type=jnp.float32)
        placing = (list_iota[:, None] == slot_set[None, :]).astype(jnp.float32)
        summed_here = jnp.dot(
            placing,
            product.reshape(group_size, tile_size * col_width),
            precision=lax.Precision.HIGHEST,
            preferred_element_type=jnp.float32,
        )
        return (running + summed_here, None)

    start = jnp.zeros((list_count, tile_size * col_width), jnp.float32)
    summed, _ = lax.scan(
        one_group,
        start,
        (
            blocks.reshape(group_total, group_size, tile_size, tile_size),
            local_cols.reshape(group_total, group_size),
            slots.reshape(group_total, group_size),
        ),
    )
    part = summed.reshape(list_count, tile_size, col_width).astype(jnp.bfloat16)
    per_owner = list_count // prow_count
    arrived, arrived_ids = (
        lax.all_to_all(
            part.reshape(prow_count, per_owner, tile_size, col_width),
            "prow",
            split_axis=0,
            concat_axis=0,
            tiled=True,
        ),
        lax.all_to_all(
            send_tiles.reshape(prow_count, per_owner),
            "prow",
            split_axis=0,
            concat_axis=0,
            tiled=True,
        ),
    )
    owned_ids = arrived_ids.reshape(-1) - (pcol_here * strip_rows + prow_here * own_count)
    placing = (jnp.arange(own_count)[:, None] == owned_ids[None, :]).astype(jnp.bfloat16)
    gathered = jnp.einsum(
        "os,spk->opk",
        placing,
        arrived.reshape(list_count, tile_size, col_width),
        preferred_element_type=jnp.float32,
    )
    patch_count = own_count * tile_size
    colour_count = albedo.shape[0]
    lit = (
        gathered.reshape(patch_count, colour_count, col_width // colour_count)
        * jnp.transpose(albedo)[:, :, None]
    )
    return (lit.reshape(patch_count, col_width) + emission.astype(jnp.float32)).astype(jnp.bfloat16)


def solution(mesh):
    placed = (
        P(("prow", "pcol"), None, None),
        P(("prow", "pcol")),
        P(("prow", "pcol")),
        P(("prow", "pcol")),
        P(("prow", "pcol"), None),
        P(None, ("pcol", "prow")),
        P(("pcol", "prow"), None),
    )
    return jax.shard_map(
        per_device, mesh=mesh, in_specs=placed, out_specs=P(("pcol", "prow"), None), check_vma=False
    )
```

profile of v0, /device:TPU:1, one launch (start us, length us, event | category | flops | bytes accessed | tf_op | source)
XLA Modules:
  0.0 804.8 jit_solution(11871469207304912627)
XLA Ops:
  8.6 4.3 all-to-all-start
  14.5 173.2 %all-gather.2.cloned.1.call-done = bf16[16384,384]{1,0:T(8,128)(2,1)} async-done(((bf16[2048,384]{1,0:T(8,128)(2,1)}), bf16[16384,384]{1,0:T(8,128)(2,1)}) %all-gather.2.cloned.1.call-update) | async-done | bytes 12582928 | tf_op jit(solution)/shard_map/all_gather | solution.py:19
  187.7 17.2 %reshape.88 = bf16[128,49152]{1,0:T(8,128)(2,1)} reshape(bf16[16384,384]{1,0:T(8,128)(2,1)} %all-gather.2.cloned.1.call-done) | data formatting | bytes 25165824 | tf_op jit(solution)/shard_map/reshape | solution.py:21
  204.9 558.7 %while.11 = (s32[]{:T(128)}, f32[16,49152]{1,0:T(8,128)S(1)}, s32[10,64]{1,0:T(8,128)S(1)}, bf16[10,64,128,128]{3,2,1,0:T(8,128)(2,1)}, s32[10,64]{1,0:T(8,128)S...) while((s32[]{:T(128)}, f32[16,49152]{1,0:T(8,128)S(1)}, s32[10,64]{1,0:T(8,128)S(1)}, ...), condition=%wide.region_2.3_spmd.clone, body=%wide.region_1.2_spmd.clone.sunk | while | flops 1414007296 | bytes 102767336 | solution.py:42
  204.9 18.6 %gather_fusion = bf16[64,49152]{1,0:T(8,128)(2,1)} fusion(bf16[128,49152]{1,0:T(8,128)(2,1)} %get-tuple-element.136, s32[1024]{0:T(1024)S(1)} %pad_clamp_fusion.2), kind=kCustom, calls=%fused_computation.clone.clone.1 | custom fusion | bytes 12583168 | tf_op jit(solution)/shard_map/while/body/eval_jaxpr/jit(_take)/gather | solution.py:30
  223.6 4.2 copy.32
  227.8 1.4 bitcast_select_fusion.2
  229.1 7.9 fusion.28
  237.0 16.3 %copy.33 = f32[8,8,128,384]{3,1,2,0:T(8,128)} copy(f32[8,8,128,384]{3,2,1,0:T(8,128)} %bitcast.59) | data formatting | bytes 25165824 | tf_op jit(solution)/shard_map/while
  253.3 7.4 convolution_add_fusion.2
  260.8 18.6 %gather_fusion = bf16[64,49152]{1,0:T(8,128)(2,1)} fusion(bf16[128,49152]{1,0:T(8,128)(2,1)} %get-tuple-element.136, s32[1024]{0:T(1024)S(1)} %pad_clamp_fusion.2), kind=kCustom, calls=%fused_computation.clone.clone.1 | custom fusion | bytes 12583168 | tf_op jit(solution)/shard_map/while/body/eval_jaxpr/jit(_take)/gather | solution.py:30
  279.4 4.2 copy.32
  283.6 1.4 bitcast_select_fusion.2
  285.0 7.9 fusion.28
  292.9 16.3 %copy.33 = f32[8,8,128,384]{3,1,2,0:T(8,128)} copy(f32[8,8,128,384]{3,2,1,0:T(8,128)} %bitcast.59) | data formatting | bytes 25165824 | tf_op jit(solution)/shard_map/while
  309.2 7.4 convolution_add_fusion.2
  316.6 18.6 %gather_fusion = bf16[64,49152]{1,0:T(8,128)(2,1)} fusion(bf16[128,49152]{1,0:T(8,128)(2,1)} %get-tuple-element.136, s32[1024]{0:T(1024)S(1)} %pad_clamp_fusion.2), kind=kCustom, calls=%fused_computation.clone.clone.1 | custom fusion | bytes 12583168 | tf_op jit(solution)/shard_map/while/body/eval_jaxpr/jit(_take)/gather | solution.py:30
  335.3 4.2 copy.32
  340.8 7.9 fusion.28
  348.7 16.3 %copy.33 = f32[8,8,128,384]{3,1,2,0:T(8,128)} copy(f32[8,8,128,384]{3,2,1,0:T(8,128)} %bitcast.59) | data formatting | bytes 25165824 | tf_op jit(solution)/shard_map/while
  365.0 7.4 convolution_add_fusion.2
  372.5 18.6 %gather_fusion = bf16[64,49152]{1,0:T(8,128)(2,1)} fusion(bf16[128,49152]{1,0:T(8,128)(2,1)} %get-tuple-element.136, s32[1024]{0:T(1024)S(1)} %pad_clamp_fusion.2), kind=kCustom, calls=%fused_computation.clone.clone.1 | custom fusion | bytes 12583168 | tf_op jit(solution)/shard_map/while/body/eval_jaxpr/jit(_take)/gather | solution.py:30
  391.1 4.2 copy.32
  395.3 1.4 bitcast_select_fusion.2
  396.7 7.9 fusion.28
  404.6 16.3 %copy.33 = f32[8,8,128,384]{3,1,2,0:T(8,128)} copy(f32[8,8,128,384]{3,2,1,0:T(8,128)} %bitcast.59) | data formatting | bytes 25165824 | tf_op jit(solution)/shard_map/while
  420.9 7.4 convolution_add_fusion.2
  428.3 18.6 %gather_fusion = bf16[64,49152]{1,0:T(8,128)(2,1)} fusion(bf16[128,49152]{1,0:T(8,128)(2,1)} %get-tuple-element.136, s32[1024]{0:T(1024)S(1)} %pad_clamp_fusion.2), kind=kCustom, calls=%fused_computation.clone.clone.1 | custom fusion | bytes 12583168 | tf_op jit(solution)/shard_map/while/body/eval_jaxpr/jit(_take)/gather | solution.py:30
  447.0 4.2 copy.32
  451.2 1.4 bitcast_select_fusion.2
  452.5 7.9 fusion.28
  460.4 16.3 %copy.33 = f32[8,8,128,384]{3,1,2,0:T(8,128)} copy(f32[8,8,128,384]{3,2,1,0:T(8,128)} %bitcast.59) | data formatting | bytes 25165824 | tf_op jit(solution)/shard_map/while
  476.7 7.4 convolution_add_fusion.2
  484.2 18.6 %gather_fusion = bf16[64,49152]{1,0:T(8,128)(2,1)} fusion(bf16[128,49152]{1,0:T(8,128)(2,1)} %get-tuple-element.136, s32[1024]{0:T(1024)S(1)} %pad_clamp_fusion.2), kind=kCustom, calls=%fused_computation.clone.clone.1 | custom fusion | bytes 12583168 | tf_op jit(solution)/shard_map/while/body/eval_jaxpr/jit(_take)/gather | solution.py:30
  502.8 4.2 copy.32
  508.4 7.9 fusion.28
  516.3 16.3 %copy.33 = f32[8,8,128,384]{3,1,2,0:T(8,128)} copy(f32[8,8,128,384]{3,2,1,0:T(8,128)} %bitcast.59) | data formatting | bytes 25165824 | tf_op jit(solution)/shard_map/while
  532.6 7.4 convolution_add_fusion.2
  540.0 18.6 %gather_fusion = bf16[64,49152]{1,0:T(8,128)(2,1)} fusion(bf16[128,49152]{1,0:T(8,128)(2,1)} %get-tuple-element.136, s32[1024]{0:T(1024)S(1)} %pad_clamp_fusion.2), kind=kCustom, calls=%fused_computation.clone.clone.1 | custom fusion | bytes 12583168 | tf_op jit(solution)/shard_map/while/body/eval_jaxpr/jit(_take)/gather | solution.py:30
  558.7 4.2 copy.32
  564.2 7.9 fusion.28
  572.1 16.3 %copy.33 = f32[8,8,128,384]{3,1,2,0:T(8,128)} copy(f32[8,8,128,384]{3,2,1,0:T(8,128)} %bitcast.59) | data formatting | bytes 25165824 | tf_op jit(solution)/shard_map/while
  588.4 7.4 convolution_add_fusion.2
  595.9 18.6 %gather_fusion = bf16[64,49152]{1,0:T(8,128)(2,1)} fusion(bf16[128,49152]{1,0:T(8,128)(2,1)} %get-tuple-element.136, s32[1024]{0:T(1024)S(1)} %pad_clamp_fusion.2), kind=kCustom, calls=%fused_computation.clone.clone.1 | custom fusion | bytes 12583168 | tf_op jit(solution)/shard_map/while/body/eval_jaxpr/jit(_take)/gather | solution.py:30
  614.5 4.2 copy.32
  620.1 7.9 fusion.28
  628.0 16.3 %copy.33 = f32[8,8,128,384]{3,1,2,0:T(8,128)} copy(f32[8,8,128,384]{3,2,1,0:T(8,128)} %bitcast.59) | data formatting | bytes 25165824 | tf_op jit(solution)/shard_map/while
  644.2 7.4 convolution_add_fusion.2
  651.7 18.6 %gather_fusion = bf16[64,49152]{1,0:T(8,128)(2,1)} fusion(bf16[128,49152]{1,0:T(8,128)(2,1)} %get-tuple-element.136, s32[1024]{0:T(1024)S(1)} %pad_clamp_fusion.2), kind=kCustom, calls=%fused_computation.clone.clone.1 | custom fusion | bytes 12583168 | tf_op jit(solution)/shard_map/while/body/eval_jaxpr/jit(_take)/gather | solution.py:30
  670.4 4.2 copy.32
  675.9 7.9 fusion.28
  683.8 16.3 %copy.33 = f32[8,8,128,384]{3,1,2,0:T(8,128)} copy(f32[8,8,128,384]{3,2,1,0:T(8,128)} %bitcast.59) | data formatting | bytes 25165824 | tf_op jit(solution)/shard_map/while
  700.1 7.4 convolution_add_fusion.2
  707.6 18.6 %gather_fusion = bf16[64,49152]{1,0:T(8,128)(2,1)} fusion(bf16[128,49152]{1,0:T(8,128)(2,1)} %get-tuple-element.136, s32[1024]{0:T(1024)S(1)} %pad_clamp_fusion.2), kind=kCustom, calls=%fused_computation.clone.clone.1 | custom fusion | bytes 12583168 | tf_op jit(solution)/shard_map/while/body/eval_jaxpr/jit(_take)/gather | solution.py:30
  726.2 4.2 copy.32
  731.8 7.9 fusion.28
  739.7 16.3 %copy.33 = f32[8,8,128,384]{3,1,2,0:T(8,128)} copy(f32[8,8,128,384]{3,2,1,0:T(8,128)} %bitcast.59) | data formatting | bytes 25165824 | tf_op jit(solution)/shard_map/while
  755.9 7.4 convolution_add_fusion.2
  764.0 2.4 copy.23
  766.4 5.4 all-to-all-start.1
  772.1 2.4 copy.26
  775.2 15.8 %all-to-all-done.1 = bf16[4,4,128,384]{3,1,2,0:T(4,128)(2,1)} async-done(((bf16[4,4,128,384]{3,1,2,0:T(4,128)(2,1)}), bf16[4,4,128,384]{3,1,2,0:T(4,128)(2,1)}, u32[]{:S(2)}, u32[]{:S(2)}) %all-to-all-start.1) | async-done | bytes 1572896 | tf_op jit(solution)/shard_map/all_to_all | solution.py:54
  791.1 1.9 copy.24
  796.3 1.6 fusion.10
  (69 shorter events, 17.0 us)
Async XLA Ops:
  6.5 181.2 %all-gather.2.cloned.1.call-start = ((), (), s32[]{:S(2)}) async-start(), calls=%async_computation.2 | async-start | bytes 14155776 | tf_op jit(solution)/shard_map/all_gather | solution.py:19
  8.6 757.8 %all-to-all-start = ((s32[4,1,4]{2,1,0:T(1,128)}), s32[4,1,4]{2,1,0:T(1,128)}, u32[]{:S(2)}, u32[]{:S(2)}) async-start(s32[4,1,4]{2,1,0:T(1,128)} %bitcast), calls=%async_computation | async-start | bytes 4096 | tf_op jit(solution)/shard_map/all_to_all | solution.py:61
  764.0 7.8 copy-start.2
  766.4 24.7 %all-to-all-start.1 = ((bf16[4,4,128,384]{3,1,2,0:T(4,128)(2,1)}), bf16[4,4,128,384]{3,1,2,0:T(4,128)(2,1)}, u32[]{:S(2)}, u32[]{:S(2)}) async-start(bf16[4,4,128,384]{3,1,2,0:T(4,128)(2,1)} %copy.23), calls=%async_computation.1 | async-start | bytes 3145728 | tf_op jit(solution)/shard_map/all_to_all | solution.py:54
  794.0 1.9 copy-start
  794.0 2.3 copy-start.1
Sparse Core Ops, SparseCore 0:
  9.5 178.0 all-gather.1
where the time goes:
time: 808 us; the launch traced here: 805 us
  local copies, waits for them, and re-layouts  420 us (52%)
  waiting for transfers between devices  190 us (24%)
  matrix products  154 us (19%)
  other arithmetic  17.8 us (2%)
  between operations  13.5 us (2%)
  starting transfers between devices  9.64 us (1%)
    while x20, local copies, waits for them, and re-layouts  204 us
    gather x10, local copies, waits for them, and re-layouts, one_group(): jnp.take(slab_flat, col_set, axis=0)  186 us
    all_gather x1, waiting for transfers between devices, per_device(): slab = lax.all_gather(lighting, 'pcol', axis=0, tiled=True)  173 us
    dot_general x10, matrix products, one_group(): jnp.einsum('gpq,gqk->gpk', block_set, picked, preferred_element_type=jnp....  79 us
    dot_general x10, matrix products, one_group(): jnp.dot(placing, product.reshape(group_size, tile_size * col_width), prec...  74.1 us
    reshape x1, local copies, waits for them, and re-layouts, per_device(): slab_flat = slab.reshape(slab_count, tile_size * col_width)  17.2 us
  transfers between devices with their start and end apart: 3, of which 2 were waited for; matrix products, arithmetic and copies ran while one was open for 72% of the time, Pallas kernels for 0%

commit v1 on v0

v1 whole, which is shorter than its diff:
```python
import functools

import jax
import jax.numpy as jnp
from jax import lax
from jax.experimental import pallas as pl
from jax.experimental.pallas import tpu as pltpu
from jax.sharding import PartitionSpec as P

GROUP = 8
MESH = pl.DeviceIdType.MESH


def ring_place(pcol, n):
    odd = pcol % 2
    return (1 - odd) * (pcol // 2) + odd * (n - 1 - pcol // 2)


def ring_device(place, n):
    late = place // (n // 2)
    return (1 - late) * (2 * place) + late * (2 * (n - 1 - place) + 1)


def fused(
    n,
    rows,
    colours,
    plan_ref,
    last_ref,
    col_ref,
    ids_ref,
    blocks_ref,
    light_ref,
    arr_ref,
    got_ref,
    *scratch,
):
    slabs = scratch[:colours]
    parts = scratch[colours : 2 * colours]
    blk, sums, ring_send, ring_recv, own_sem, blk_sem, ex_send, ex_recv, ex_own, id_send, id_recv, id_own = scratch[
        2 * colours :
    ]
    count = blocks_ref.shape[0]
    groups = plan_ref.shape[1]
    tiles = light_ref.shape[0]
    half = tiles // 2
    listed = last_ref.shape[0]
    per = listed // rows
    basis = slabs[0].shape[2]
    prow = lax.axis_index("prow")
    pcol = lax.axis_index("pcol")
    place = ring_place(pcol, n)
    after = ring_device((place + 1) % n, n)
    before = ring_device((place + n - 1) % n, n)
    messages = n - 1

    barrier = pltpu.get_barrier_semaphore()
    for side in (after, before):
        pl.semaphore_signal(barrier, inc=1, device_id={"pcol": side}, device_id_type=MESH)
    for d in range(1, rows):
        pl.semaphore_signal(barrier, inc=1, device_id={"prow": (prow + d) % rows}, device_id_type=MESH)

    own = [
        pltpu.make_async_copy(
            light_ref.at[:, :, pl.ds(c * basis, basis)], slabs[c].at[pl.ds(pcol * tiles, tiles)], own_sem.at[c]
        )
        for c in range(colours)
    ]
    for copy in own:
        copy.start()
    pl.semaphore_wait(barrier, 2 + rows - 1)

    def piece(c, m, way, arriving):
        step = m // 2
        part = (m + way) % 2
        if way == 0:
            source = (place + n - step - arriving) % n
        else:
            source = (place + step + arriving) % n
        at = ring_device(source, n) * tiles + part * half
        window = slabs[c].at[pl.ds(at, half)]
        return pltpu.make_async_remote_copy(
            src_ref=window,
            dst_ref=window,
            send_sem=ring_send.at[way, c, m],
            recv_sem=ring_recv.at[way, c, m],
            device_id={"pcol": before if way else after},
            device_id_type=MESH,
        )

    def to_row(c, d):
        target = (prow + d) % rows
        return pltpu.make_async_remote_copy(
            src_ref=parts[c].at[pl.ds(target * per, per)],
            dst_ref=arr_ref.at[c, prow],
            send_sem=ex_send.at[c, d],
            recv_sem=ex_recv.at[c, d],
            device_id={"prow": target},
            device_id_type=MESH,
        )

    def from_row(c, d):
        origin = (prow + rows - d) % rows
        return pltpu.make_async_remote_copy(
            src_ref=parts[c].at[pl.ds(0, per)],
            dst_ref=arr_ref.at[c, origin],
            send_sem=ex_send.at[c, d],
            recv_sem=ex_recv.at[c, d],
            device_id={"prow": origin},
            device_id_type=MESH,
        )

    def ids_to(d):
        target = (prow + d) % rows
        return pltpu.make_async_remote_copy(
            src_ref=ids_ref,
            dst_ref=got_ref.at[prow],
            send_sem=id_send.at[d],
            recv_sem=id_recv.at[d],
            device_id={"prow": target},
            device_id_type=MESH,
        )

    def ids_from(d):
        origin = (prow + rows - d) % rows
        return pltpu.make_async_remote_copy(
            src_ref=ids_ref,
            dst_ref=got_ref.at[origin],
            send_sem=id_send.at[d],
            recv_sem=id_recv.at[d],
            device_id={"prow": origin},
            device_id_type=MESH,
        )

    load = pltpu.make_async_copy(blocks_ref, blk.at[pl.ds(0, count)], blk_sem)

    def compute(c, low, high):
        def one(i, running):
            base = plan_ref[0, i]
            end = plan_ref[1, i]
            keep = plan_ref[2, i].astype(jnp.float32)
            left, right = [], []
            for j in range(GROUP):
                at = base + j
                inside = at < end
                left.append(blk[jnp.where(inside, at, count)])
                right.append(slabs[c][col_ref[jnp.where(inside, at, 0)]])
            running = running * keep + jnp.dot(
                jnp.concatenate(left, axis=1),
                jnp.concatenate(right, axis=0),
                preferred_element_type=jnp.float32,
            )
            sums[i + 1] = running
            return running

        lax.fori_loop(low, high, one, sums[low])

    def exchange(c):
        for s in range(listed):
            parts[c][s] = sums[last_ref[s]].astype(jnp.bfloat16)
        for d in range(1, rows):
            to_row(c, d).start()
        pltpu.make_async_copy(parts[c].at[pl.ds(prow * per, per)], arr_ref.at[c, prow], ex_own.at[c]).start()

    def finish_ring(c):
        for m in range(max(messages - 2, 0), messages):
            for way in (0, 1):
                piece(c, m, way, 1).wait_recv()

    cuts = [groups * k // (messages - 1) for k in range(messages)]
    for c in range(colours):
        own[c].wait()
        for m in range(messages):
            for way in (0, 1):
                if m >= 2:
                    piece(c, m - 2, way, 1).wait_recv()
                piece(c, m, way, 0).start()
            if c == 0 and m == 1:
                load.start()
                blk[count] = jnp.zeros(blk.shape[1:], blk.dtype)
                sums[0] = jnp.zeros(sums.shape[1:], sums.dtype)
                for d in range(1, rows):
                    ids_to(d).start()
                pltpu.make_async_copy(ids_ref, got_ref.at[prow], id_own).start()
            if c >= 1 and m >= 1:
                if m == 1:
                    if c == 1:
                        load.wait()
                    finish_ring(c - 1)
                compute(c - 1, cuts[m - 1], cuts[m])
                if m == messages - 1:
                    exchange(c - 1)
    finish_ring(colours - 1)
    compute(colours - 1, 0, groups)
    exchange(colours - 1)
    for c in range(colours):
        for m in range(messages):
            for way in (0, 1):
                piece(c, m, way, 0).wait_send()
        for d in range(1, rows):
            to_row(c, d).wait_send()
            from_row(c, d).wait_recv()
        pltpu.make_async_copy(parts[c].at[pl.ds(prow * per, per)], arr_ref.at[c, prow], ex_own.at[c]).wait()
    for d in range(1, rows):
        ids_to(d).wait_send()
        ids_from(d).wait_recv()
    pltpu.make_async_copy(ids_ref, got_ref.at[prow], id_own).wait()


def finish(share, here_ref, arr_ref, albedo_ref, emission_ref, out_ref, total):
    colours, rows, per = arr_ref.shape[:3]
    step = pl.program_id(0)
    total[...] = jnp.zeros_like(total)
    for r in range(rows):
        for k in range(per):
            at = here_ref[r * per + k] - step * share

            @pl.when(jnp.logical_and(at >= 0, at < share))
            def _():
                for c in range(colours):
                    total[c, at] += arr_ref[c, r, k].astype(jnp.float32)

    basis = total.shape[3]
    for t in range(share):
        factor = albedo_ref[t]
        for c in range(colours):
            lane = slice(c * basis, (c + 1) * basis)
            out_ref[t, :, lane] = (
                total[c, t] * factor[:, c : c + 1] + emission_ref[t, :, lane].astype(jnp.float32)
            ).astype(out_ref.dtype)


def per_device(blocks, row_index, col_index, send_tiles, lighting, albedo, emission):
    count, tile = blocks.shape[:2]
    width = lighting.shape[1]
    colours = albedo.shape[0]
    basis = width // colours
    listed = send_tiles.shape[0]
    rows = lax.axis_size("prow")
    n = lax.axis_size("pcol")
    tiles = lighting.shape[0] // tile
    owned = emission.shape[0] // tile
    per = listed // rows
    prow = lax.axis_index("prow")
    pcol = lax.axis_index("pcol")
    groups = (count + listed * (GROUP - 1)) // GROUP

    first = jnp.sum((row_index[None, :] < send_tiles[:, None]).astype(jnp.int32), axis=1)
    past = jnp.sum((row_index[None, :] <= send_tiles[:, None]).astype(jnp.int32), axis=1)
    needed = (past - first + GROUP - 1) // GROUP
    order = jnp.arange(listed)
    ends = jnp.sum(jnp.where(order[None, :] <= order[:, None], needed[None, :], 0), axis=1)
    starts = ends - needed
    index = jnp.arange(groups)[:, None]
    inside = jnp.logical_and(index >= starts[None, :], index < ends[None, :])
    base = jnp.sum(jnp.where(inside, first[None, :] + (index - starts[None, :]) * GROUP, 0), axis=1)
    limit = jnp.sum(jnp.where(inside, past[None, :], 0), axis=1)
    keep = jnp.sum(jnp.where(jnp.logical_and(inside, index > starts[None, :]), 1, 0), axis=1)
    plan = jnp.stack([base, limit, keep])
    local_cols = col_index - prow * (n * tiles)
    ids = jnp.broadcast_to(jnp.pad(send_tiles, (0, 128 - listed))[None, :], (8, 128))

    half = tile * basis
    slab_bytes = n * tiles * half * 2 * colours
    vmem = (count + 1) * tile * tile * 2 + slab_bytes + (groups + 1) * half * 4 + colours * listed * half * 2
    smem = pl.BlockSpec(memory_space=pltpu.SMEM)
    hbm = pl.BlockSpec(memory_space=pl.ANY)
    arrived, got = pl.pallas_call(
        functools.partial(fused, n, rows, colours),
        out_shape=(
            jax.ShapeDtypeStruct((colours, rows, per, tile, basis), jnp.bfloat16),
            jax.ShapeDtypeStruct((rows, 8, 128), jnp.int32),
        ),
        in_specs=[smem, smem, smem, hbm, hbm, hbm],
        out_specs=(hbm, hbm),
        scratch_shapes=[pltpu.VMEM((n * tiles, tile, basis), jnp.bfloat16) for _ in range(colours)]
        + [pltpu.VMEM((listed, tile, basis), jnp.bfloat16) for _ in range(colours)]
        + [
            pltpu.VMEM((count + 1, tile, tile), jnp.bfloat16),
            pltpu.VMEM((groups + 1, tile, basis), jnp.float32),
            pltpu.SemaphoreType.DMA((2, colours, n - 1)),
            pltpu.SemaphoreType.DMA((2, colours, n - 1)),
            pltpu.SemaphoreType.DMA((colours,)),
            pltpu.SemaphoreType.DMA,
            pltpu.SemaphoreType.DMA((colours, rows)),
            pltpu.SemaphoreType.DMA((colours, rows)),
            pltpu.SemaphoreType.DMA((colours,)),
            pltpu.SemaphoreType.DMA((rows,)),
            pltpu.SemaphoreType.DMA((rows,)),
            pltpu.SemaphoreType.DMA,
        ],
        compiler_params=pltpu.CompilerParams(
            collective_id=0, has_side_effects=True, vmem_limit_bytes=vmem + (2 << 20)
        ),
        cost_estimate=pl.CostEstimate(
            flops=2 * count * tile * tile * width, bytes_accessed=count * tile * tile * 2 + slab_bytes, transcendentals=0
        ),
    )(
        plan,
        ends,
        local_cols,
        ids,
        blocks,
        lighting.reshape(tiles, tile, width),
    )

    mine = lax.dynamic_slice_in_dim(got[:, 0, :], prow * per, per, axis=1)
    here = mine.reshape(-1) - (pcol * rows + prow) * owned
    share = 4
    out = pl.pallas_call(
        functools.partial(finish, share),
        out_shape=jax.ShapeDtypeStruct((owned, tile, width), jnp.bfloat16),
        grid=(owned // share,),
        in_specs=[
            smem,
            pl.BlockSpec(arrived.shape, lambda i: (0, 0, 0, 0, 0)),
            pl.BlockSpec((share, tile, colours), lambda i: (i, 0, 0)),
            pl.BlockSpec((share, tile, width), lambda i: (i, 0, 0)),
        ],
        out_specs=pl.BlockSpec((share, tile, width), lambda i: (i, 0, 0)),
        scratch_shapes=[pltpu.VMEM((colours, share, tile, basis), jnp.float32)],
        compiler_params=pltpu.CompilerParams(vmem_limit_bytes=24 << 20),
    )(
        here,
        arrived,
        jnp.transpose(albedo).reshape(owned, tile, colours),
        emission.reshape(owned, tile, width),
    )
    return out.reshape(owned * tile, width)


def solution(mesh):
    placed = (
        P(("prow", "pcol"), None, None),
        P(("prow", "pcol")),
        P(("prow", "pcol")),
        P(("prow", "pcol")),
        P(("prow", "pcol"), None),
        P(None, ("pcol", "prow")),
        P(("pcol", "prow"), None),
    )
    return jax.shard_map(
        per_device, mesh=mesh, in_specs=placed, out_specs=P(("pcol", "prow"), None), check_vma=False
    )
```

time: 808 us -> 164 us (0.20)
  local copies, waits for them, and re-layouts: 420 us -> 5.82 us
  waiting for transfers between devices: 190 us -> 0 us
  Pallas kernels: 0 us -> 156 us
  matrix products: 154 us -> 0 us
  other arithmetic: 17.8 us -> 1.9 us
  between operations: 13.5 us -> 0.06 us
  starting transfers between devices: 9.64 us -> 0 us
    while x20 -> x0, local copies, waits for them, and re-layouts: 204 us -> none
    gather x10 -> x0, local copies, waits for them, and re-layouts: 186 us -> none  [one_group(): jnp.take(slab_flat, col_set, axis=0)]
    all_gather x1 -> x0, waiting for transfers between devices: 173 us -> none  [per_device(): slab = lax.all_gather(lighting, 'pcol', axis=0, tiled=True)]
    pallas_call x0 -> x2, Pallas kernels: none -> 156 us  [the longest x1 152 us: per_device(): pl.pallas_call(functools.partial(fused, n, rows, colours), out_shape=(jax...]
    dot_general x21 -> x0, matrix products: 154 us -> none  [the longest x10 79 us: one_group(): jnp.einsum('gpq,gqk->gpk', block_set, picked, preferred_element_type=jnp....]
    reshape x4 -> x0, local copies, waits for them, and re-layouts: 17.7 us -> none  [the longest x1 17.2 us: per_device(): slab_flat = slab.reshape(slab_count, tile_size * col_width)]
    all_to_all x2 -> x0, waiting for transfers between devices: 15.8 us -> none  [the longest x1 15.8 us: per_device(): lax.all_to_all(part.reshape(prow_count, per_owner, tile_size, col_width),...]
    select_n x20 -> x1, other arithmetic: 13.7 us -> 0.01 us  [per_device(): needed = (past - first + GROUP - 1) // GROUP]
  transfers between devices with their start and end apart: 3 -> 0, of which waited for: 2 -> 0; matrix products, arithmetic and copies ran while one was open for 72% -> 0% of each run, Pallas kernels for 0% -> 0%
where the time goes in v1:
time: 164 us
  Pallas kernels  156 us (95%)
  local copies, waits for them, and re-layouts  5.82 us (4%)
  other arithmetic  1.9 us (1%)
    pallas_call x1, Pallas kernels, per_device(): pl.pallas_call(functools.partial(fused, n, rows, colours), out_shape=(jax...  152 us
    unnamed x8, local copies, waits for them, and re-layouts  3.96 us
    pallas_call x1, Pallas kernels, per_device(): pl.pallas_call(functools.partial(finish, share), out_shape=jax.ShapeDtype...  3.68 us

profile of v1, /device:TPU:1, one launch (start us, length us, event | category | flops | bytes accessed | tf_op | source)
XLA Modules:
  0.0 163.9 jit_solution(12956939297417710598)
XLA Ops:
  0.0 0.7 pad.4
  0.7 0.9 convert_reduce_fusion
  1.6 0.1 select_reduce_fusion.3.last_ref
  1.7 0.1 select_reduce_fusion.2
  1.8 0.7 broadcast_subtract_fusion.col_ref
  2.5 1.1 copy.9
  3.6 0.0 copy-start.3
  3.6 1.4 copy-done.3
  5.0 0.0 copy-start
  5.0 152.5 %shard_map.73 = (bf16[3,4,4,128,128]{4,3,2,1,0:T(8,128)(2,1)S(1)}, s32[4,8,128]{2,1,0:T(8,128)S(1)}) custom-call(s32[3,94]{1,0:T(4,128)S(1)} %pad_add_fusion.plan_ref, s32[16]{0:T(128)S(1)} %select_reduce_fusion.3.last_ref, s32[640]{0:T(1024)S(1)} %broadcast_subtract_fusion.col_ref, s32[8,128]{1,0:T(8,128)S(1)} %broadcast_in_dim.39.ids_ref, ...), custom_call_target="tpu_custom_call" | custom-call | flops 8053063680 | bytes 33554432 | tf_op jit(solution)/shard_map/pallas_call | solution.py:268
  157.5 0.0 copy-start.1
  157.5 1.1 copy-done.1
  158.7 0.1 subtract_reduce_fusion
  158.7 0.1 sub.59.here_ref
  158.8 0.0 copy-done
  158.8 0.0 copy-start.2
  158.8 1.4 copy-done.2
  160.2 3.7 %shard_map.74 = bf16[16,128,384]{2,1,0:T(8,128)(2,1)} custom-call(s32[16]{0:T(128)S(1)} %sub.59.here_ref, bf16[3,4,4,128,128]{4,3,2,1,0:T(8,128)(2,1)S(1)} %copy-done.2, f32[16,128,3]{2,1,0:T(8,128)S(1)} %bitcast.8, bf16[16,128,384]{2,1,0:T(8,128)(2,1)S(1)} %bitcast.9), custom_call_target="tpu_custom_call" | custom-call | tf_op jit(solution)/shard_map/pallas_call | solution.py:310
  (5 shorter events, 0.0 us)
Async XLA Ops:
  3.6 1.4 copy-start.3
  5.0 153.8 %copy-start = (bf16[2048,384]{1,0:T(8,128)(2,1)S(1)}, bf16[2048,384]{1,0:T(8,128)(2,1)}, u32[]{:S(2)}) copy-start(bf16[2048,384]{1,0:T(8,128)(2,1)} %param.13) | copy-start | bytes 4718596
  157.5 1.1 copy-start.1
  158.8 1.4 copy-start.2

commit v2 on v1

--- a/solution.py
+++ b/solution.py
@@ -8,6 +8,7 @@
 from jax.sharding import PartitionSpec as P
 
 GROUP = 8
+BATCH = 8
 MESH = pl.DeviceIdType.MESH
 
 
@@ -136,24 +137,29 @@
 
     def compute(c, low, high):
         def one(i, running):
-            base = plan_ref[0, i]
-            end = plan_ref[1, i]
-            keep = plan_ref[2, i].astype(jnp.float32)
-            left, right = [], []
-            for j in range(GROUP):
-                at = base + j
-                inside = at < end
-                left.append(blk[jnp.where(inside, at, count)])
-                right.append(slabs[c][col_ref[jnp.where(inside, at, 0)]])
-            running = running * keep + jnp.dot(
-                jnp.concatenate(left, axis=1),
-                jnp.concatenate(right, axis=0),
-                preferred_element_type=jnp.float32,
-            )
-            sums[i + 1] = running
+            products = []
+            for u in range(BATCH):
+                base = plan_ref[0, i * BATCH + u]
+                end = plan_ref[1, i * BATCH + u]
+                left, right = [], []
+                for j in range(GROUP):
+                    at = base + j
+                    inside = at < end
+                    left.append(blk[jnp.where(inside, at, count)])
+                    right.append(slabs[c][col_ref[jnp.where(inside, at, 0)]])
+                products.append(
+                    jnp.dot(
+                        jnp.concatenate(left, axis=1),
+                        jnp.concatenate(right, axis=0),
+                        preferred_element_type=jnp.float32,
+                    )
+                )
+            for u in range(BATCH):
+                running = running * plan_ref[2, i * BATCH + u].astype(jnp.float32) + products[u]
+                sums[i * BATCH + u + 1] = running
             return running
 
-        lax.fori_loop(low, high, one, sums[low])
+        lax.fori_loop(low, high, one, sums[low * BATCH])
 
     def exchange(c):
         for s in range(listed):
@@ -167,7 +173,8 @@
             for way in (0, 1):
                 piece(c, m, way, 1).wait_recv()
 
-    cuts = [groups * k // (messages - 1) for k in range(messages)]
+    batches = groups // BATCH
+    cuts = [batches * k // (messages - 1) for k in range(messages)]
     for c in range(colours):
         own[c].wait()
         for m in range(messages):
@@ -191,7 +198,7 @@
                 if m == messages - 1:
                     exchange(c - 1)
     finish_ring(colours - 1)
-    compute(colours - 1, 0, groups)
+    compute(colours - 1, 0, batches)
     exchange(colours - 1)
     for c in range(colours):
         for m in range(messages):
@@ -244,6 +251,7 @@
     prow = lax.axis_index("prow")
     pcol = lax.axis_index("pcol")
     groups = (count + listed * (GROUP - 1)) // GROUP
+    groups = -(-groups // BATCH) * BATCH
 
     first = jnp.sum((row_index[None, :] < send_tiles[:, None]).astype(jnp.int32), axis=1)
     past = jnp.sum((row_index[None, :] <= send_tiles[:, None]).astype(jnp.int32), axis=1)
@@ -290,7 +298,7 @@
             pltpu.SemaphoreType.DMA,
         ],
         compiler_params=pltpu.CompilerParams(
-            collective_id=0, has_side_effects=True, vmem_limit_bytes=vmem + (2 << 20)
+            collective_id=0, has_side_effects=True, vmem_limit_bytes=max(vmem + (2 << 20), 58 << 20)
         ),
         cost_estimate=pl.CostEstimate(
             flops=2 * count * tile * tile * width, bytes_accessed=count * tile * tile * 2 + slab_bytes, transcendentals=0

time: 164 us -> 152 us (0.927)
  Pallas kernels: 156 us -> 144 us
    pallas_call x1, Pallas kernels: 152 us -> 140 us  [per_device(): pl.pallas_call(functools.partial(fused, n, rows, colours), out_shape=(jax...]
    unnamed x8 -> x6, local copies, waits for them, and re-layouts: 3.96 us -> 1.42 us
where the time goes in v2:
time: 152 us; the launch traced here: 151 us
  Pallas kernels  144 us (95%)
  local copies, waits for them, and re-layouts  4.59 us (3%)
  other arithmetic  3.05 us (2%)
    pallas_call x1, Pallas kernels, per_device(): pl.pallas_call(functools.partial(fused, n, rows, colours), out_shape=(jax...  140 us
    pallas_call x1, Pallas kernels, per_device(): pl.pallas_call(functools.partial(finish, share), out_shape=jax.ShapeDtype...  3.68 us

profile of v2, /device:TPU:1, one launch (start us, length us, event | category | flops | bytes accessed | tf_op | source)
XLA Modules:
  0.0 151.4 jit_solution(4463366115949274530)
XLA Ops:
  0.0 0.7 pad.4
  0.7 0.9 convert_reduce_fusion
  1.6 0.1 select_reduce_fusion.3.last_ref
  1.7 0.0 copy-start.2
  1.7 0.1 select_reduce_fusion.2
  1.8 0.6 pad_add_fusion.plan_ref
  2.4 0.6 broadcast_in_dim.39.ids_ref
  3.0 1.3 broadcast_subtract_fusion.col_ref
  4.2 1.1 copy.9
  5.4 0.0 copy-done.2
  5.4 0.0 copy-start
  5.4 140.0 %shard_map.73 = (bf16[3,4,4,128,128]{4,3,2,1,0:T(8,128)(2,1)}, s32[4,8,128]{2,1,0:T(8,128)}) custom-call(s32[3,96]{1,0:T(4,128)} %pad_add_fusion.plan_ref, s32[16]{0:T(128)} %copy-done.2, s32[640]{0:T(1024)} %broadcast_subtract_fusion.col_ref, s32[8,128]{1,0:T(8,128)} %broadcast_in_dim.39.ids_ref, bf16[640,128,128]{2,1,0:T(8,128)(2,1)} %blocks_ref.1, ...), custom_call_target="tpu_custom_call" | custom-call | flops 8053063680 | bytes 33554432 | tf_op jit(solution)/shard_map/pallas_call | solution.py:276
  145.4 0.7 slice.3
  146.1 0.1 subtract_reduce_fusion
  146.2 0.1 sub.59.here_ref
  146.3 0.0 copy-done
  146.3 0.0 copy-start.1
  146.3 1.4 copy-done.1
  147.7 3.7 %shard_map.74 = bf16[16,128,384]{2,1,0:T(8,128)(2,1)} custom-call(s32[16]{0:T(128)S(1)} %sub.59.here_ref, bf16[3,4,4,128,128]{4,3,2,1,0:T(8,128)(2,1)S(1)} %copy-done.1, f32[16,128,3]{2,1,0:T(8,128)S(1)} %bitcast.8, bf16[16,128,384]{2,1,0:T(8,128)(2,1)S(1)} %bitcast.9), custom_call_target="tpu_custom_call" | custom-call | tf_op jit(solution)/shard_map/pallas_call | solution.py:318
  (2 shorter events, 0.0 us)
Async XLA Ops:
  1.7 3.7 %copy-start.2 = (s32[16]{0:T(128)}, s32[16]{0:T(128)S(1)}, u32[]{:S(2)}) copy-start(s32[16]{0:T(128)S(1)} %select_reduce_fusion.3.last_ref) | copy-start | bytes 196
  5.4 140.9 %copy-start = (bf16[2048,384]{1,0:T(8,128)(2,1)S(1)}, bf16[2048,384]{1,0:T(8,128)(2,1)}, u32[]{:S(2)}) copy-start(bf16[2048,384]{1,0:T(8,128)(2,1)} %param.13) | copy-start | bytes 4718596
  146.3 1.4 copy-start.1

commit v3 on v2

--- a/solution.py
+++ b/solution.py
@@ -214,27 +214,20 @@
     pltpu.make_async_copy(ids_ref, got_ref.at[prow], id_own).wait()
 
 
-def finish(share, here_ref, arr_ref, albedo_ref, emission_ref, out_ref, total):
-    colours, rows, per = arr_ref.shape[:3]
+def finish(here_ref, arr_ref, albedo_ref, emission_ref, out_ref, total):
+    rows, per = arr_ref.shape[1:3]
     step = pl.program_id(0)
     total[...] = jnp.zeros_like(total)
     for r in range(rows):
         for k in range(per):
-            at = here_ref[r * per + k] - step * share
-
-            @pl.when(jnp.logical_and(at >= 0, at < share))
-            def _():
-                for c in range(colours):
-                    total[c, at] += arr_ref[c, r, k].astype(jnp.float32)
-
-    basis = total.shape[3]
-    for t in range(share):
-        factor = albedo_ref[t]
-        for c in range(colours):
-            lane = slice(c * basis, (c + 1) * basis)
-            out_ref[t, :, lane] = (
-                total[c, t] * factor[:, c : c + 1] + emission_ref[t, :, lane].astype(jnp.float32)
-            ).astype(out_ref.dtype)
+            total[here_ref[r * per + k]] += arr_ref[0, r, k].astype(jnp.float32)
+    for c in range(albedo_ref.shape[2]):
+
+        @pl.when(step == c)
+        def _():
+            for t in range(total.shape[0]):
+                lit = total[t] * albedo_ref[t][:, c : c + 1] + emission_ref[t].astype(jnp.float32)
+                out_ref[t] = lit.astype(out_ref.dtype)
 
 
 def per_device(blocks, row_index, col_index, send_tiles, lighting, albedo, emission):
@@ -314,19 +307,18 @@
 
     mine = lax.dynamic_slice_in_dim(got[:, 0, :], prow * per, per, axis=1)
     here = mine.reshape(-1) - (pcol * rows + prow) * owned
-    share = 4
     out = pl.pallas_call(
-        functools.partial(finish, share),
+        finish,
         out_shape=jax.ShapeDtypeStruct((owned, tile, width), jnp.bfloat16),
-        grid=(owned // share,),
+        grid=(colours,),
         in_specs=[
             smem,
-            pl.BlockSpec(arrived.shape, lambda i: (0, 0, 0, 0, 0)),
-            pl.BlockSpec((share, tile, colours), lambda i: (i, 0, 0)),
-            pl.BlockSpec((share, tile, width), lambda i: (i, 0, 0)),
+            pl.BlockSpec((1, rows, per, tile, basis), lambda i: (i, 0, 0, 0, 0)),
+            pl.BlockSpec((owned, tile, colours), lambda i: (0, 0, 0)),
+            pl.BlockSpec((owned, tile, basis), lambda i: (0, 0, i)),
         ],
-        out_specs=pl.BlockSpec((share, tile, width), lambda i: (i, 0, 0)),
-        scratch_shapes=[pltpu.VMEM((colours, share, tile, basis), jnp.float32)],
+        out_specs=pl.BlockSpec((owned, tile, basis), lambda i: (0, 0, i)),
+        scratch_shapes=[pltpu.VMEM((owned, tile, basis), jnp.float32)],
         compiler_params=pltpu.CompilerParams(vmem_limit_bytes=24 << 20),
     )(
         here,

time: 152 us -> 151 us (level)
  no operation moved by 1% of the time
where the time goes in v3:
time: 151 us
  Pallas kernels  143 us (95%)
  local copies, waits for them, and re-layouts  4.59 us (3%)
  other arithmetic  3.05 us (2%)
    pallas_call x1, Pallas kernels, per_device(): pl.pallas_call(functools.partial(fused, n, rows, colours), out_shape=(jax...  140 us
    pallas_call x1, Pallas kernels, per_device(): pl.pallas_call(finish, out_shape=jax.ShapeDtypeStruct((owned, tile, width...  3.33 us

profile of v3, /device:TPU:1, one launch (start us, length us, event | category | flops | bytes accessed | tf_op | source)
XLA Modules:
  0.0 151.0 jit_solution(3707248376778271251)
XLA Ops:
  0.0 0.7 pad.4
  0.7 0.9 convert_reduce_fusion
  1.6 0.1 select_reduce_fusion.3.last_ref
  1.7 0.0 copy-start.2
  1.7 0.1 select_reduce_fusion.2
  1.8 0.6 pad_add_fusion.plan_ref
  2.4 0.6 broadcast_in_dim.39.ids_ref
  3.0 1.3 broadcast_subtract_fusion.col_ref
  4.2 1.1 copy.9
  5.4 0.0 copy-done.2
  5.4 0.0 copy-start
  5.4 140.0 %shard_map.73 = (bf16[3,4,4,128,128]{4,3,2,1,0:T(8,128)(2,1)}, s32[4,8,128]{2,1,0:T(8,128)}) custom-call(s32[3,96]{1,0:T(4,128)} %pad_add_fusion.plan_ref, s32[16]{0:T(128)} %copy-done.2, s32[640]{0:T(1024)} %broadcast_subtract_fusion.col_ref, s32[8,128]{1,0:T(8,128)} %broadcast_in_dim.39.ids_ref, bf16[640,128,128]{2,1,0:T(8,128)(2,1)} %blocks_ref.1, ...), custom_call_target="tpu_custom_call" | custom-call | flops 8053063680 | bytes 33554432 | tf_op jit(solution)/shard_map/pallas_call | solution.py:269
  145.4 0.7 slice.3
  146.1 0.1 subtract_reduce_fusion
  146.2 0.1 sub.59.here_ref
  146.3 0.0 copy-done
  146.3 0.0 copy-start.1
  146.3 1.4 copy-done.1
  147.7 3.3 %shard_map.74 = bf16[16,128,384]{2,1,0:T(8,128)(2,1)} custom-call(s32[16]{0:T(128)S(1)} %sub.59.here_ref, bf16[3,4,4,128,128]{4,3,2,1,0:T(8,128)(2,1)S(1)} %copy-done.1, f32[16,128,3]{2,1,0:T(8,128)S(1)} %bitcast.8, bf16[16,128,384]{2,1,0:T(8,128)(2,1)S(1)} %bitcast.9), custom_call_target="tpu_custom_call" | custom-call | tf_op jit(solution)/shard_map/pallas_call | solution.py:310
  (2 shorter events, 0.0 us)
Async XLA Ops:
  1.7 3.7 %copy-start.2 = (s32[16]{0:T(128)}, s32[16]{0:T(128)S(1)}, u32[]{:S(2)}) copy-start(s32[16]{0:T(128)S(1)} %select_reduce_fusion.3.last_ref) | copy-start | bytes 196
  5.4 140.9 %copy-start = (bf16[2048,384]{1,0:T(8,128)(2,1)S(1)}, bf16[2048,384]{1,0:T(8,128)(2,1)}, u32[]{:S(2)}) copy-start(bf16[2048,384]{1,0:T(8,128)(2,1)} %param.13) | copy-start | bytes 4718596
  146.3 1.4 copy-start.1
